TPU v7x, 512 devices: a whole 4x8x8 slice. The times are simulated.
512 devices in a mesh: expert: 128 (over z, y, core), dp: 4 (over x).
Axes of the slice: x: 4, y: 8, z: 8, core: 2. Of those that a mesh axis runs over, the one named last changes fastest.
Arguments:
- tokens: bfloat16 [65536, 7168], P(('expert', 'dp')), may hold values from -6 to 6
- expert_ids: int32 [65536, 8], P(('expert', 'dp')), may hold values from 0 to 255, all different within a row; in each aligned block of 128 rows (0 to 127, 128 to 255, ...) at most 8 rows name the same one
- weight_cols: bfloat16 [256, 1024, 640], P('expert', 'dp'), may hold values from -12 to 12
- uinv_panel: float32 [256, 128, 128], P('expert'), as said below
- u_window: float32 [256, 128, 512], P('expert'), may hold values from -0.5 to 0.5
- panel_index: int32 [1], replicated, may hold values from 0 to 51
Outputs:
- q_panel: bfloat16 [256, 1024, 128], P('expert', 'dp')
- w_window: bfloat16 [256, 1024, 512], P('expert', 'dp')
- hess_grad: float32 [256, 1024, 640], P('expert', 'dp')
Inputs may be any that keep to these rules, and one draw needn't show every extreme that they name: `expert_ids`: each row names 8 different experts; within the rows of one device no expert is named by more than 8 rows, a bound that the rows of some device reach; every expert is named by some row. `uinv_panel`: each block is upper triangular, with diagonal entries from 1 to 3.
All inputs are finite; a program needn't handle non-finite values.
Results may differ from a plain program's by a relative error of at most 0.013.
Values may be sent and summed in bfloat16 or wider, within the bound.
A program may use at most 64 MiB of HBM per device.

v0:
```python
import math

import jax
import jax.numpy as jnp
from jax import lax
from jax.sharding import PartitionSpec as P

PANEL = 128


TWO_PI = 2.0 * math.pi
HIGHEST = lax.Precision.HIGHEST


def gram_matrix(routed_rows):
    return jnp.einsum(
        "simc,simd->icd", routed_rows, routed_rows, preferred_element_type=jnp.float32
    )


def pooled(pieces):
    routed_rows, counts = pieces
    totals = lax.psum((gram_matrix(routed_rows), jnp.sum(counts.astype(jnp.float32), axis=0)), "dp")
    return totals


def per_device(tokens, expert_ids, weight_cols, uinv_panel, u_window, panel_index):
    tok_rows, top_k = expert_ids.shape
    n_owner = lax.axis_size("expert")
    per_owner = weight_cols.shape[0]
    n_experts = n_owner * per_owner
    capacity = max(8, 2 * tok_rows * top_k // n_experts)
    columns = weight_cols.shape[2]
    first_col = panel_index[0] * PANEL
    window = lax.dynamic_slice_in_dim(tokens, first_col, columns, 1)
    flat_ids = expert_ids.reshape(-1)
    onehot = (flat_ids[:, None] == jnp.arange(n_experts, dtype=jnp.int32)[None, :]).astype(
        jnp.int32
    )
    slot_rank = jnp.sum((jnp.cumsum(onehot, axis=0) - onehot) * onehot, axis=1)
    slot_index = flat_ids * capacity + slot_rank
    pair_token = jnp.arange(tok_rows * top_k, dtype=jnp.int32) // top_k
    slot_token = jnp.zeros((n_experts * capacity,), jnp.int32).at[slot_index].set(pair_token)
    slot_live = jnp.zeros((n_experts * capacity,), jnp.bool_).at[slot_index].set(True)
    outgoing = jnp.where(slot_live[:, None], window[slot_token], jnp.zeros((), jnp.bfloat16))
    outgoing = outgoing.reshape(n_owner, per_owner, capacity, columns)
    sent_counts = jnp.sum(onehot, axis=0).reshape(n_owner, per_owner).astype(jnp.bfloat16)
    gram_sum, count_sum = pooled(
        (
            lax.all_to_all(outgoing, "expert", split_axis=0, concat_axis=0, tiled=True),
            lax.all_to_all(sent_counts, "expert", split_axis=0, concat_axis=0, tiled=True),
        )
    )
    hessian = gram_sum / count_sum[:, None, None]
    weights = weight_cols.astype(jnp.float32)
    panel_cols = weights[:, :, :PANEL]
    row_scale = (jnp.max(jnp.abs(panel_cols), axis=2, keepdims=True) + 1e-06) / 7.0
    scaled = panel_cols / row_scale
    quantized = row_scale * (scaled - jnp.sin(TWO_PI * scaled) / TWO_PI)
    quant_error = panel_cols - quantized
    left_part = jnp.einsum("erp,epq->erq", quant_error, uinv_panel, precision=HIGHEST)
    correction = jnp.einsum("erq,eqw->erw", left_part, u_window, precision=HIGHEST)
    change_all = jnp.concatenate([-quant_error, -correction], axis=2)
    hess_grad = jnp.einsum("erc,ecd->erd", change_all, hessian, precision=HIGHEST)
    return (
        quantized.astype(jnp.bfloat16),
        (weights[:, :, PANEL:] - correction).astype(jnp.bfloat16),
        hess_grad,
    )


def solution(mesh):
    placed = (
        P(("expert", "dp"), None),
        P(("expert", "dp"), None),
        P("expert", "dp", None),
        P("expert", None, None),
        P("expert", None, None),
        P(),
    )
    return jax.shard_map(
        per_device,
        mesh=mesh,
        in_specs=placed,
        out_specs=(P("expert", "dp", None), P("expert", "dp", None), P("expert", "dp", None)),
        check_vma=False,
    )
```

profile of v0, /device:TPU:1, one launch (start us, length us, event | category | flops | bytes accessed | tf_op | source)
XLA Modules:
  0.0 215.2 jit_solution(8948397730426357512)
XLA Ops:
  7.2 0.9 copy.15
  8.3 0.7 broadcast_multiply_fusion
  9.1 0.2 fusion.9
  9.5 0.3 copy.18
  10.0 0.4 convert_reduce_fusion
  10.5 4.3 %scatter_custom_fusion.1 = s32[2048]{0:T(1024)S(1)} fusion(s32[1024]{0:T(1024)S(1)} %bitcast.19, s32[1024]{0:T(1024)S(1)} %add_select_fusion, s32[]{:T(128)} %constant.43.clone.1), kind=kCustom, calls=%fused_computation.39 | custom fusion | bytes 8196 | tf_op jit(solution)/shard_map/scatter | solution.py:43
  15.5 4.3 %scatter_custom_fusion = pred[2048]{0:T(1024)(128)(4,1)S(1)} fusion(s32[1024]{0:T(1024)S(1)} %bitcast.20, pred[1024]{0:T(1024)(128)(4,1)S(1)} %broadcast.84, pred[]{:T(512)} %constant.41.clone.1), kind=kCustom, calls=%fused_computation.42 | custom fusion | bytes 2049 | tf_op jit(solution)/shard_map/scatter | solution.py:44
  19.8 0.2 broadcast_in_dim.31
  20.0 9.3 %gather_fusion = bf16[2048,640]{1,0:T(8,128)(2,1)} fusion(bf16[128,640]{1,0:T(8,128)(2,1)S(1)} %constant_dynamic-slice_fusion, s32[2048]{0:T(1024)S(1)} %fusion.14), kind=kCustom, calls=%fused_computation | custom fusion | bytes 5251072 | tf_op jit(solution)/shard_map/gather | solution.py:45
  29.4 2.0 broadcast_select_fusion
  31.4 80.0 %all_to_all.11 = bf16[128,2,8,640]{3,2,1,0:T(8,128)(2,1)S(1)} all-to-all(bf16[128,2,8,640]{3,2,1,0:T(8,128)(2,1)S(1)} %broadcast_select_fusion), channel_id=1, replica_groups=mesh['expert'=128,'dp'=4] {'expert'}, dimensions={0} | all-to-all | bytes 5242880 | tf_op jit(solution)/shard_map/all_to_all | solution.py:50
  111.4 4.1 %convolution_bitcast_fusion = f32[2,640,640]{2,1,0:T(8,128)} fusion(bf16[128,2,8,640]{3,2,1,0:T(8,128)(2,1)S(1)} %all_to_all.11), kind=kOutput, calls=%fused_computation.6 | convolution fusion | flops 1677721600 | bytes 5898240 | tf_op jit(solution)/shard_map/simc,simd->icd/dot_general | solution.py:16
  115.5 0.8 convert_element_type.41
  116.3 9.9 %all-to-all-start.1 = ((bf16[128,1,2]{2,1,0:T(2,128)(2,1)}), bf16[128,1,2]{2,1,0:T(2,128)(2,1)S(1)}, u32[]{:S(2)}, u32[]{:S(2)}) async-start(bf16[128,1,2]{2,1,0:T(2,128)(2,1)} %convert_element_type.41), calls=%async_computation.1 | async-start | bytes 131072 | tf_op jit(solution)/shard_map/all_to_all | solution.py:51
  126.2 1.3 convert_element_type.33
  127.5 0.1 abs_reduce_fusion
  127.7 1.6 fusion.13
  129.3 3.2 %fusion.24 = (f32[2,256,512]{2,1,0:T(8,128)}, bf16[2,256,512]{2,1,0:T(8,128)(2,1)}) fusion(f32[2,256,640]{2,1,0:T(8,128)S(1)} %convert_element_type.33, f32[2,256,128]{2,1,0:T(8,128)S(1)} %fusion.13, f32[2,128,512]{2,1,0:T(8,128)} %param.10), kind=kOutput, calls=%fused_computation.49 | convolution fusion | flops 403439616 | bytes 3407872 | tf_op jit(solution)/shard_map/erq,eqw->erw/dot_general | solution.py:62
  132.5 5.1 %all-to-all-done.1 = bf16[128,1,2]{2,1,0:T(2,128)(2,1)S(1)} async-done(((bf16[128,1,2]{2,1,0:T(2,128)(2,1)}), bf16[128,1,2]{2,1,0:T(2,128)(2,1)S(1)}, u32[]{:S(2)}, u32[]{:S(2)}) %all-to-all-start.1) | async-done | bytes 544 | tf_op jit(solution)/shard_map/all_to_all | solution.py:51
  137.6 0.2 convert_reduce_fusion.1
  137.7 1.7 fusion.12
  139.4 9.7 %psum.15 = f32[2]{0:T(128)S(1)} all-reduce(f32[2]{0:T(128)S(1)} %convert_reduce_fusion.1), channel_id=1, replica_groups=mesh['expert'=128,'dp'=4] {'dp'}, use_global_device_ids=true, to_apply=%region_9.10 | all-reduce | flops 2 | bytes 16 | tf_op jit(solution)/shard_map/psum | solution.py:23
  149.1 52.0 %all-reduce.2.cloned.1.call-done = f32[2,640,640]{2,1,0:T(8,128)} async-done(((f32[2,640,640]{2,1,0:T(8,128)}), f32[2,640,640]{2,1,0:T(8,128)}) %all-reduce.2.cloned.1.call-update) | async-done | bytes 3276816 | tf_op jit(solution)/shard_map/psum | solution.py:23
  201.1 7.2 %fusion = f32[2,256,640]{2,1,0:T(8,128)} fusion(f32[2,640,640]{2,1,0:T(8,128)} %all-reduce.2.cloned.1.call-done, f32[2]{0:T(128)S(1)} %psum.15, f32[2,256,512]{2,1,0:T(8,128)} %get-tuple-element.7, f32[2,256,128]{2,1,0:T(8,128)S(1)} %get-tuple-element.5), kind=kOutput, calls=%fused_computation.3 | convolution fusion | flops 2517729280 | bytes 5898248 | tf_op jit(solution)/shard_map/erc,ecd->erd/dot_general | solution.py:64
  (22 shorter events, 0.7 us)
Async XLA Ops:
  7.2 12.8 %copy-start = (bf16[128,7168]{1,0:T(8,128)(2,1)S(1)}, bf16[128,7168]{1,0:T(8,128)(2,1)}, u32[]{:S(2)}) copy-start(bf16[128,7168]{1,0:T(8,128)(2,1)} %param.6) | copy-start | bytes 5505028
  7.2 193.9 %all-reduce.2.cloned.1.call-start = ((), (), s32[]{:S(2)}) async-start(), calls=%async_computation.2 | async-start | bytes 6553600 | tf_op jit(solution)/shard_map/psum | solution.py:23
  115.5 12.2 %copy-start.1 = (f32[2,128,128]{2,1,0:T(8,128)S(1)}, f32[2,128,128]{2,1,0:T(8,128)}, u32[]{:S(2)}) copy-start(f32[2,128,128]{2,1,0:T(8,128)} %param.9) | copy-start | bytes 393220
  116.3 21.3 %all-to-all-start.1 = ((bf16[128,1,2]{2,1,0:T(2,128)(2,1)}), bf16[128,1,2]{2,1,0:T(2,128)(2,1)S(1)}, u32[]{:S(2)}, u32[]{:S(2)}) async-start(bf16[128,1,2]{2,1,0:T(2,128)(2,1)} %convert_element_type.41), calls=%async_computation.1 | async-start | bytes 131072 | tf_op jit(solution)/shard_map/all_to_all | solution.py:51
Sparse Core Ops, SparseCore 0:
  115.6 85.4 all-reduce.1
where the time goes:
time: 216 us; the launch traced here: 215 us
  blocking collectives  89.8 us (42%)
  waiting for transfers between devices  57.1 us (26%)
  local copies, waits for them, and re-layouts  20.8 us (10%)
  matrix products  16.1 us (7%)
  between operations  14.9 us (7%)
  starting transfers between devices  9.92 us (5%)
  other arithmetic  6.66 us (3%)
    all_to_all x1, blocking collectives, per_device(): lax.all_to_all(outgoing, 'expert', split_axis=0, concat_axis=0, tiled=True)  80 us
    psum x1, waiting for transfers between devices, pooled(): lax.psum((gram_matrix(routed_rows), jnp.sum(counts.astype(jnp.float32), a...  52 us
    all_to_all x1, starting transfers between devices, per_device(): lax.all_to_all(sent_counts, 'expert', split_axis=0, concat_axis=0, tiled=...  9.88 us
    psum x1, blocking collectives, pooled(): lax.psum((gram_matrix(routed_rows), jnp.sum(counts.astype(jnp.float32), a...  9.74 us
    gather x1, local copies, waits for them, and re-layouts, per_device(): window[slot_token]  9.32 us
    dot_general x1, matrix products, per_device(): jnp.einsum('erc,ecd->erd', change_all, hessian, precision=HIGHEST)  7.23 us
    all_to_all x1, waiting for transfers between devices, per_device(): lax.all_to_all(sent_counts, 'expert', split_axis=0, concat_axis=0, tiled=...  5.12 us
    scatter x1, local copies, waits for them, and re-layouts, per_device(): jnp.zeros((n_experts * capacity,), jnp.bool_).at[slot_index].set(True)  4.34 us
  transfers between devices with their start and end apart: 2, of which 2 were waited for; matrix products, arithmetic and copies ran while one was open for 4% of the time, Pallas kernels for 0%

commit v1 on v0

v1 whole, which is shorter than its diff:
```python
import functools
import math

import jax
import jax.numpy as jnp
from jax import lax
from jax.experimental import pallas as pl
from jax.experimental.pallas import tpu as pltpu
from jax.sharding import PartitionSpec as P

PANEL = 128
SLOTS = 8
TWO_PI = 2.0 * math.pi
HIGHEST = lax.Precision.HIGHEST
MESH = pl.DeviceIdType.MESH
F32 = jnp.float32
BF16 = jnp.bfloat16


def sin_turn(turns):
    part = turns - jnp.round(turns)
    half = jnp.where(part < 0, -0.5, 0.5)
    part = jnp.where(jnp.abs(part) > 0.25, half - part, part)
    angle = part * TWO_PI
    square = angle * angle
    series = jnp.full_like(square, -1.0 / math.factorial(11))
    for power in (9, 7, 5, 3, 1):
        sign = 1.0 if power % 4 == 1 else -1.0
        series = series * square + sign / math.factorial(power)
    return angle * series


def kernel(
    line, n_dp,
    win_ref, ids_ref, w_ref, uinv_ref, uw_ref,
    q_ref, ww_ref, hg_ref,
    tok, idb, outb, inb, cnt_out, cnt_in, change, gram_out, gram_in, whole, hess,
    tok_s, tok_r, ids_s, ids_r, row_s, row_r, cnt_s, cnt_r, rs_s, rs_r, ag_s, ag_r,
):
    idx = lax.axis_index("expert")
    xpos = lax.axis_index("dp")
    core = idx % 2
    y = (idx // 2) % line
    z = idx // (2 * line)
    dests = 2 * line
    pairs = line // 2
    blocks = w_ref.shape[2] // PANEL
    upper = [(b, c) for b in range(blocks) for c in range(b, blocks)]
    part_rows = PANEL // n_dp
    body = len(upper) * part_rows
    tokens = win_ref.shape[0]

    stride1 = 2 * line - (2 * line - 2) * core
    place1 = z * (1 - core) + y * core
    base1 = idx - place1 * stride1
    stride2 = 2 + (2 * line - 2) * core
    place2 = y * (1 - core) + z * core
    base2 = idx - core - place2 * stride2
    self_dest = 2 * place2 + core
    my_slot = core * line + place2

    barrier = pltpu.get_barrier_semaphore()

    def greet(device, at=xpos):
        pl.semaphore_signal(barrier, inc=1, device_id=(device, at), device_id_type=MESH)

    @pl.loop(1, line)
    def _(d):
        greet(base1 + ((place1 + d) % line) * stride1)

    @pl.loop(1, line)
    def _(d):
        greet(base2 + ((place2 + d) % line) * stride2 + core)

    @pl.loop(0, line)
    def _(d):
        other = 1 - core
        stride = 2 + (2 * line - 2) * other
        place = y * (1 - other) + z * other
        greet(idx - core - place * stride + d * stride + other)

    @pl.loop(1, n_dp)
    def _(d):
        greet(idx, (xpos + d) % n_dp)

    pl.semaphore_wait(barrier, 3 * line - 2 + n_dp - 1)

    @pl.loop(1, line)
    def _(d):
        peer = (base1 + ((place1 + d) % line) * stride1, xpos)
        pltpu.make_async_remote_copy(
            ids_ref, idb.at[place1], ids_s, ids_r.at[place1], device_id=peer, device_id_type=MESH
        ).start()
        pltpu.make_async_remote_copy(
            win_ref, tok.at[place1], tok_s, tok_r.at[place1], device_id=peer, device_id_type=MESH
        ).start()

    tok[place1] = win_ref[...]
    idb[place1] = ids_ref[...]

    for i in range(2):
        panel = w_ref[i, :, :PANEL].astype(F32)
        scale = (jnp.max(jnp.abs(panel), axis=1, keepdims=True) + 1e-6) / 7.0
        error = scale * sin_turn(panel / scale) * (1.0 / TWO_PI)
        q_ref[i] = (panel - error).astype(BF16)
        change[i, :, :PANEL] = (-error).astype(BF16)
        left = jnp.dot(error, uinv_ref[i], precision=HIGHEST, preferred_element_type=F32)
        correction = jnp.dot(left, uw_ref[i], precision=HIGHEST, preferred_element_type=F32)
        ww_ref[i] = (w_ref[i, :, PANEL:].astype(F32) - correction).astype(BF16)
        change[i, :, PANEL:] = (-correction).astype(BF16)

    row = lax.broadcasted_iota(jnp.int32, (2 * dests, 2 * tokens), 0)
    named = (
        (row // 4) * (4 + (4 * line - 4) * core)
        + row % 4
        + (1 - core) * z * (4 * line)
        + core * y * 4
    )
    before = (
        lax.broadcasted_iota(jnp.int32, (2 * tokens, 2 * tokens), 0)
        < lax.broadcasted_iota(jnp.int32, (2 * tokens, 2 * tokens), 1)
    ).astype(F32).astype(BF16)
    slot = lax.broadcasted_iota(jnp.int32, (2 * SLOTS, 2 * tokens), 0).astype(F32)
    cnt_out[...] = jnp.zeros_like(cnt_out)

    def send_rows(i, k, q):
        d = (self_dest + k) % dests
        peer = (base2 + (d // 2) * stride2 + d % 2, xpos)
        if q is None:
            src, dst = outb.at[i, d], inb.at[i, my_slot]
        else:
            src, dst = outb.at[i, d, q], inb.at[i, my_slot, q]
        pltpu.make_async_remote_copy(
            src, dst, row_s.at[i], row_r.at[i], device_id=peer, device_id_type=MESH
        ).start()

    @pl.loop(0, pairs)
    def _(t):
        q = (place1 // 2 + t) % pairs
        for s in range(2):
            j = 2 * q + s

            @pl.when(j != place1)
            def _():
                pltpu.make_async_copy(ids_ref, idb.at[j], ids_r.at[j]).wait()
                pltpu.make_async_copy(win_ref, tok.at[j], tok_r.at[j]).wait()

        ids = jnp.concatenate([idb[2 * q], idb[2 * q + 1]], axis=1)
        member = jnp.zeros(named.shape, F32)
        for k in range(ids.shape[0]):
            member = member + jnp.where(ids[k : k + 1, :] == named, 1.0, 0.0)
        rank = jnp.dot(member.astype(BF16), before, preferred_element_type=F32)
        rank = jnp.where(member > 0.5, rank, -1.0)
        half = member[:, :tokens] + member[:, tokens:]
        cnt_out[...] += jnp.broadcast_to(half[:, None, :], cnt_out.shape)
        source = tok[pl.ds(2 * q, 2)].reshape(2 * tokens, win_ref.shape[1])
        step = min(8, 2 * dests)
        for e in range(0, 2 * dests, step):
            pick = jnp.where(rank[e : e + step, None, :] == slot[None], 1.0, 0.0)
            pick = pick.reshape(step * 2 * SLOTS, 2 * tokens).astype(BF16)
            rows = jnp.dot(pick, source, preferred_element_type=F32).astype(BF16)
            rows = rows.reshape(step, 2 * SLOTS, -1)
            for m in range(step):
                outb[(e + m) % 2, (e + m) // 2, q] = rows[m]
        inb[0, my_slot, q] = outb[0, self_dest, q]
        inb[1, my_slot, q] = outb[1, self_dest, q]

        @pl.loop(1, dests)
        def _(k):
            send_rows(0, k, q)

    @pl.loop(1, dests)
    def _(k):
        d = (self_dest + k) % dests
        peer = (base2 + (d // 2) * stride2 + d % 2, xpos)
        pltpu.make_async_remote_copy(
            cnt_out.at[pl.ds(2 * d, 2)], cnt_in.at[my_slot], cnt_s, cnt_r,
            device_id=peer, device_id_type=MESH,
        ).start()
        send_rows(1, k, None)

    cnt_in[my_slot] = cnt_out[pl.ds(2 * self_dest, 2)]

    def rows_wait(i):
        view = inb.at[i, pl.ds(0, dests - 1)]
        pltpu.make_async_copy(view, view, row_r.at[i]).wait()

    def gram(i):
        rows_wait(i)
        held = inb.at[i]
        rows = held[...].reshape(-1, w_ref.shape[2])
        for b in range(blocks):
            product = lax.dot_general(
                rows[:, b * PANEL : (b + 1) * PANEL], rows[:, b * PANEL :],
                (((0,), (0,)), ((), ())), preferred_element_type=F32,
            ).astype(BF16)
            for c in range(b, blocks):
                t = upper.index((b, c))
                for p in range(n_dp):
                    gram_out[i, p, t * part_rows : (t + 1) * part_rows, :] = product[
                        p * part_rows : (p + 1) * part_rows,
                        (c - b) * PANEL : (c - b + 1) * PANEL,
                    ]
        count = jnp.sum(cnt_in[:, i], axis=0)[:1]
        count = jnp.broadcast_to(count, (16, PANEL)).astype(BF16)
        for p in range(n_dp):
            gram_out[i, p, body:, :] = count
        for d in range(1, n_dp):
            other = (xpos + d) % n_dp
            pltpu.make_async_remote_copy(
                gram_out.at[i, other], gram_in.at[i, d - 1], rs_s.at[i, d - 1], rs_r.at[i, d - 1],
                device_id=(idx, other), device_id_type=MESH,
            ).start()

    def share(i):
        for d in range(1, n_dp):
            pltpu.make_async_copy(gram_in.at[i, d - 1], gram_in.at[i, d - 1], rs_r.at[i, d - 1]).wait()
        total = gram_out[i, xpos].astype(F32)
        for d in range(1, n_dp):
            total = total + gram_in[i, d - 1].astype(F32)
        whole[i, xpos] = total[:body].astype(BF16)
        for d in range(1, n_dp):
            other = (xpos + d) % n_dp
            pltpu.make_async_remote_copy(
                whole.at[i, xpos], whole.at[i, xpos], ag_s.at[i, d - 1], ag_r.at[i, xpos],
                device_id=(idx, other), device_id_type=MESH,
            ).start()
        return 1.0 / jnp.sum(total[body : body + 1], axis=1, keepdims=True)

    def finish(i, inverse):
        for d in range(1, n_dp):
            other = (xpos + d) % n_dp
            pltpu.make_async_copy(whole.at[i, other], whole.at[i, other], ag_r.at[i, other]).wait()
        for t, (b, c) in enumerate(upper):
            for p in range(n_dp):
                hess[b * PANEL + p * part_rows : b * PANEL + (p + 1) * part_rows,
                     c * PANEL : (c + 1) * PANEL] = whole[i, p, t * part_rows : (t + 1) * part_rows, :]
        for c in range(blocks):
            low, high = c * PANEL, (c + 1) * PANEL
            out = jnp.dot(change[i, :, :high], hess[:high, low:high], preferred_element_type=F32)
            if high < w_ref.shape[2]:
                out = out + lax.dot_general(
                    change[i, :, high:], hess[low:high, high:],
                    (((1,), (1,)), ((), ())), preferred_element_type=F32,
                )
            hg_ref[i, :, low:high] = out * inverse

    pltpu.make_async_copy(cnt_in.at[pl.ds(0, dests - 1)], cnt_in.at[pl.ds(0, dests - 1)], cnt_r).wait()
    gram(0)
    inverse0 = share(0)
    finish(0, inverse0)
    gram(1)
    inverse1 = share(1)
    finish(1, inverse1)

    for i in range(2):
        view = outb.at[i, pl.ds(0, dests - 1)]
        pltpu.make_async_copy(view, view, row_s.at[i]).wait()
        for d in range(n_dp - 1):
            pltpu.make_async_copy(gram_in.at[i, d], gram_in.at[i, d], rs_s.at[i, d]).wait()
            pltpu.make_async_copy(whole.at[i, 0], whole.at[i, 0], ag_s.at[i, d]).wait()
    view = cnt_in.at[pl.ds(0, dests - 1)]
    pltpu.make_async_copy(view, view, cnt_s).wait()
    view = tok.at[pl.ds(0, line - 1)]
    pltpu.make_async_copy(view, view, tok_s).wait()
    view = idb.at[pl.ds(0, line - 1)]
    pltpu.make_async_copy(view, view, ids_s).wait()


def per_device(tokens, expert_ids, weight_cols, uinv_panel, u_window, panel_index):
    n_expert, n_dp = lax.axis_size("expert"), lax.axis_size("dp")
    line = math.isqrt(n_expert // 2)
    dests = 2 * line
    rows, columns = weight_cols.shape[1:]
    n_tok, top_k = expert_ids.shape
    window = lax.dynamic_slice_in_dim(tokens, panel_index[0] * PANEL, columns, 1)
    blocks = columns // PANEL
    body = blocks * (blocks + 1) // 2 * (PANEL // n_dp)
    dma = pltpu.SemaphoreType.DMA
    vmem = pl.BlockSpec(memory_space=pltpu.VMEM)
    return pl.pallas_call(
        functools.partial(kernel, line, n_dp),
        out_shape=(
            jax.ShapeDtypeStruct((2, rows, PANEL), BF16),
            jax.ShapeDtypeStruct((2, rows, columns - PANEL), BF16),
            jax.ShapeDtypeStruct((2, rows, columns), F32),
        ),
        in_specs=[vmem] * 5,
        out_specs=(vmem,) * 3,
        scratch_shapes=[
            pltpu.VMEM((line, n_tok, columns), BF16),
            pltpu.VMEM((line, top_k, n_tok), jnp.int32),
            pltpu.VMEM((2, dests, line // 2, 2 * SLOTS, columns), BF16),
            pltpu.VMEM((2, dests, line // 2, 2 * SLOTS, columns), BF16),
            pltpu.VMEM((2 * dests, 8, n_tok), F32),
            pltpu.VMEM((dests, 2, 8, n_tok), F32),
            pltpu.VMEM((2, rows, columns), BF16),
            pltpu.VMEM((2, n_dp, body + 16, PANEL), BF16),
            pltpu.VMEM((2, n_dp - 1, body + 16, PANEL), BF16),
            pltpu.VMEM((2, n_dp, body, PANEL), BF16),
            pltpu.VMEM((columns, columns), BF16),
            dma, dma((line,)), dma, dma((line,)), dma((2,)), dma((2,)), dma, dma,
            dma((2, n_dp - 1)), dma((2, n_dp - 1)), dma((2, n_dp - 1)), dma((2, n_dp)),
        ],
        compiler_params=pltpu.CompilerParams(
            collective_id=0, has_side_effects=True, vmem_limit_bytes=56 * 1024 * 1024
        ),
    )(window, expert_ids.T, weight_cols, uinv_panel, u_window)


def solution(mesh):
    placed = (
        P(("expert", "dp"), None),
        P(("expert", "dp"), None),
        P("expert", "dp", None),
        P("expert", None, None),
        P("expert", None, None),
        P(),
    )
    return jax.shard_map(
        per_device,
        mesh=mesh,
        in_specs=placed,
        out_specs=(P("expert", "dp", None), P("expert", "dp", None), P("expert", "dp", None)),
        check_vma=False,
    )
```

time: 216 us -> 108 us (0.50)
  Pallas kernels: 0 us -> 99.8 us
  blocking collectives: 89.8 us -> 0 us
  waiting for transfers between devices: 57.1 us -> 0 us
  matrix products: 16.1 us -> 0 us
  local copies, waits for them, and re-layouts: 20.8 us -> 6.01 us
  between operations: 14.9 us -> 1.44 us
  starting transfers between devices: 9.92 us -> 0 us
  other arithmetic: 6.66 us -> 0 us
    pallas_call x0 -> x1, Pallas kernels: none -> 99.8 us  [per_device(): pl.pallas_call(functools.partial(kernel, line, n_dp), out_shape=(jax.Shap...]
    all_to_all x1 -> x0, blocking collectives: 80 us -> none  [per_device(): lax.all_to_all(outgoing, 'expert', split_axis=0, concat_axis=0, tiled=True)]
    psum x1 -> x0, waiting for transfers between devices: 52 us -> none  [pooled(): lax.psum((gram_matrix(routed_rows), jnp.sum(counts.astype(jnp.float32), a...]
    dot_general x4 -> x0, matrix products: 16.1 us -> none  [the longest x1 7.23 us: per_device(): jnp.einsum('erc,ecd->erd', change_all, hessian, precision=HIGHEST)]
    all_to_all x1 -> x0, starting transfers between devices: 9.88 us -> none  [per_device(): lax.all_to_all(sent_counts, 'expert', split_axis=0, concat_axis=0, tiled=...]
    psum x1 -> x0, blocking collectives: 9.74 us -> none  [pooled(): lax.psum((gram_matrix(routed_rows), jnp.sum(counts.astype(jnp.float32), a...]
    gather x1 -> x0, local copies, waits for them, and re-layouts: 9.32 us -> none  [per_device(): window[slot_token]]
    scatter x2 -> x0, local copies, waits for them, and re-layouts: 8.66 us -> none  [the longest x1 4.34 us: per_device(): jnp.zeros((n_experts * capacity,), jnp.bool_).at[slot_index].set(True)]
  transfers between devices with their start and end apart: 2 -> 0, of which waited for: 2 -> 0; matrix products, arithmetic and copies ran while one was open for 4% -> 0% of each run, Pallas kernels for 0% -> 0%
where the time goes in v1:
time: 108 us; the launch traced here: 107 us
  Pallas kernels  99.8 us (92%)
  local copies, waits for them, and re-layouts  6.01 us (6%)
  between operations  1.44 us (1%)
    pallas_call x1, Pallas kernels, per_device(): pl.pallas_call(functools.partial(kernel, line, n_dp), out_shape=(jax.Shap...  99.8 us
    unnamed x7, local copies, waits for them, and re-layouts  5.33 us

profile of v1, /device:TPU:1, one launch (start us, length us, event | category | flops | bytes accessed | tf_op | source)
XLA Modules:
  0.0 107.3 jit_solution(17334412623402694178)
XLA Ops:
  0.6 0.0 copy-start
  1.4 0.7 copy-done
  2.2 0.7 constant_dynamic-slice_fusion.win_ref
  2.8 99.8 %shard_map.85 = (bf16[2,256,128]{2,1,0:T(8,128)(2,1)}, bf16[2,256,512]{2,1,0:T(8,128)(2,1)}, f32[2,256,640]{2,1,0:T(8,128)}) custom-call(bf16[128,640]{1,0:T(8,128)(2,1)} %constant_dynamic-slice_fusion.win_ref, s32[8,128]{1,0:T(8,128)} %bitcast.2, bf16[2,256,640]{2,1,0:T(8,128)(2,1)} %w_ref.1, f32[2,128,128]{2,1,0:T(8,128)} %uinv_ref.1, f32[2,128,512]{2,1,0:T(8,128)} %uw_ref.1), custom_call_target="tpu_custom_call" | custom-call | tf_op jit(solution)/shard_map/pallas_call | solution.py:281
  102.7 0.0 copy-start.1
  102.7 1.7 %copy.13 = bf16[2,256,128]{2,1,0:T(8,128)(2,1)} copy(bf16[2,256,128]{2,1,0:T(8,128)(2,1)} %get-tuple-element.6) | data formatting | bytes 262144
  104.4 1.9 %copy.14 = bf16[2,256,512]{2,1,0:T(8,128)(2,1)} copy(bf16[2,256,512]{2,1,0:T(8,128)(2,1)} %get-tuple-element.7) | data formatting | bytes 1048576
  106.2 0.0 copy-done.1
  106.2 1.1 copy.15
Async XLA Ops:
  0.6 1.5 %copy-start = (bf16[128,7168]{1,0:T(8,128)(2,1)S(1)}, bf16[128,7168]{1,0:T(8,128)(2,1)}, u32[]{:S(2)}) copy-start(bf16[128,7168]{1,0:T(8,128)(2,1)} %param.6) | copy-start | bytes 5505028
  102.7 3.6 %copy-start.1 = (f32[2,256,640]{2,1,0:T(8,128)S(1)}, f32[2,256,640]{2,1,0:T(8,128)}, u32[]{:S(2)}) copy-start(f32[2,256,640]{2,1,0:T(8,128)} %get-tuple-element.8) | copy-start | bytes 3932164

commit v2 on v1

v2 whole, which is shorter than its diff:
```python
import functools
import math

import jax
import jax.numpy as jnp
from jax import lax
from jax.experimental import pallas as pl
from jax.experimental.pallas import tpu as pltpu
from jax.sharding import PartitionSpec as P

PANEL = 128
SLOTS = 8
TWO_PI = 2.0 * math.pi
HIGHEST = lax.Precision.HIGHEST
MESH = pl.DeviceIdType.MESH
F32 = jnp.float32
BF16 = jnp.bfloat16


def sin_turn(turns):
    part = turns - jnp.round(turns)
    half = jnp.where(part < 0, -0.5, 0.5)
    part = jnp.where(jnp.abs(part) > 0.25, half - part, part)
    angle = part * TWO_PI
    square = angle * angle
    series = jnp.full_like(square, -1.0 / math.factorial(11))
    for power in (9, 7, 5, 3, 1):
        sign = 1.0 if power % 4 == 1 else -1.0
        series = series * square + sign / math.factorial(power)
    return angle * series


def upper_tiles(blocks):
    return [(b, c) for b in range(blocks) for c in range(b, blocks)]


def route_kernel(
    line, n_dp,
    win_ref, ids_ref, w_hbm, uinv_hbm, uw_hbm,
    change, whole, total_cnt,
    w_ref, uinv_ref, uw_ref, tok, idb, outb, inb, cnt_out, cnt_in, gram_out, gram_in,
    load_s, tok_s, tok_r, ids_s, ids_r, row_s, row_r, cnt_s, cnt_r, rs_s, rs_r, ag_s, ag_r,
):
    idx = lax.axis_index("expert")
    xpos = lax.axis_index("dp")
    core = idx % 2
    y = (idx // 2) % line
    z = idx // (2 * line)
    dests = 2 * line
    pairs = line // 2
    columns = w_ref.shape[2]
    blocks = columns // PANEL
    upper = upper_tiles(blocks)
    part_rows = PANEL // n_dp
    body = len(upper) * part_rows
    tokens = tok.shape[1]
    own = line - 2

    loads = [
        pltpu.make_async_copy(w_hbm, w_ref, load_s.at[0]),
        pltpu.make_async_copy(uinv_hbm, uinv_ref, load_s.at[1]),
        pltpu.make_async_copy(uw_hbm, uw_ref, load_s.at[2]),
    ]
    for load in loads:
        load.start()

    stride1 = 2 * line - (2 * line - 2) * core
    place1 = z * (1 - core) + y * core
    base1 = idx - place1 * stride1
    stride2 = 2 + (2 * line - 2) * core
    place2 = y * (1 - core) + z * core
    base2 = idx - core - place2 * stride2
    self_dest = 2 * place2 + core
    my_slot = core * line + place2

    barrier = pltpu.get_barrier_semaphore()

    def greet(device, at=xpos):
        pl.semaphore_signal(barrier, inc=1, device_id=(device, at), device_id_type=MESH)

    @pl.loop(1, line)
    def _(d):
        greet(base1 + ((place1 + d) % line) * stride1)

    @pl.loop(1, line)
    def _(d):
        greet(base2 + ((place2 + d) % line) * stride2 + core)

    @pl.loop(0, line)
    def _(d):
        other = 1 - core
        stride = 2 + (2 * line - 2) * other
        place = y * (1 - other) + z * other
        greet(idx - core - place * stride + d * stride + other)

    @pl.loop(1, n_dp)
    def _(d):
        greet(idx, (xpos + d) % n_dp)

    tok[own] = win_ref[...]
    idb[own] = ids_ref[...]

    pl.semaphore_wait(barrier, 3 * line - 2 + n_dp - 1)

    right = (base1 + ((place1 + 1) % line) * stride1, xpos)
    left = (base1 + ((place1 + line - 1) % line) * stride1, xpos)

    for step in range(1, pairs + 1):
        for way in range(1 if step == pairs else 2):
            slot = 2 * (step - 1) + way + (1 if step == pairs else 0)
            at = (place1 + (step if way == 0 else line - step)) % line
            pltpu.make_async_remote_copy(
                ids_ref, idb.at[slot], ids_s, ids_r.at[slot],
                device_id=(base1 + at * stride1, xpos), device_id_type=MESH,
            ).start()

    def hop(source, target, way, far):
        rows = pl.ds(way * (tokens // 2), tokens // 2) if far else pl.ds(0, tokens)
        sem = 2 * pairs - 2 + way if far else target
        return pltpu.make_async_remote_copy(
            tok.at[source, rows], tok.at[target, rows], tok_s.at[sem], tok_r.at[sem],
            device_id=right if way == 0 else left, device_id_type=MESH,
        )

    hops = []

    def start_hops(step):
        for way in range(2):
            far = step == pairs
            source = own if step == 1 else 2 * (step - 2) + way
            copy = hop(source, line - 1 if far else 2 * (step - 1) + way, way, far)
            copy.start()
            hops.append(copy)

    start_hops(1)

    def weights(i):
        panel = w_ref[i, :, :PANEL].astype(F32)
        scale = (jnp.max(jnp.abs(panel), axis=1, keepdims=True) + 1e-6) / 7.0
        error = scale * sin_turn(panel / scale) * (1.0 / TWO_PI)
        change[i, :, :PANEL] = (-error).astype(BF16)
        left_part = jnp.dot(error, uinv_ref[i], precision=HIGHEST, preferred_element_type=F32)
        correction = jnp.dot(left_part, uw_ref[i], precision=HIGHEST, preferred_element_type=F32)
        change[i, :, PANEL:] = (-correction).astype(BF16)

    row = lax.broadcasted_iota(jnp.int32, (2 * dests, 2 * tokens), 0)
    named = (
        (row // 4) * (4 + (4 * line - 4) * core)
        + row % 4
        + (1 - core) * z * (4 * line)
        + core * y * 4
    )
    before = (
        lax.broadcasted_iota(jnp.int32, (2 * tokens, 2 * tokens), 0)
        < lax.broadcasted_iota(jnp.int32, (2 * tokens, 2 * tokens), 1)
    ).astype(F32).astype(BF16)
    slot_of = lax.broadcasted_iota(jnp.int32, (2 * SLOTS, 2 * tokens), 0).astype(F32)
    cnt_out[...] = jnp.zeros_like(cnt_out)

    def send_rows(i, k, q):
        d = (self_dest + k) % dests
        peer = (base2 + (d // 2) * stride2 + d % 2, xpos)
        if q is None:
            src, dst = outb.at[i, d], inb.at[i, my_slot]
        else:
            src, dst = outb.at[i, d, q], inb.at[i, my_slot, q]
        pltpu.make_async_remote_copy(
            src, dst, row_s.at[i], row_r.at[i], device_id=peer, device_id_type=MESH
        ).start()

    def pick_rows(q):
        ids = jnp.concatenate([idb[2 * q], idb[2 * q + 1]], axis=1)
        member = jnp.zeros(named.shape, F32)
        for k in range(ids.shape[0]):
            member = member + jnp.where(ids[k : k + 1, :] == named, 1.0, 0.0)
        rank = jnp.dot(member.astype(BF16), before, preferred_element_type=F32)
        rank = jnp.where(member > 0.5, rank, -1.0)
        half = member[:, :tokens] + member[:, tokens:]
        cnt_out[...] += jnp.broadcast_to(half[:, None, :], cnt_out.shape)
        source = tok[pl.ds(2 * q, 2)].reshape(2 * tokens, columns)
        step = min(8, 2 * dests)
        for e in range(0, 2 * dests, step):
            pick = jnp.where(rank[e : e + step, None, :] == slot_of[None], 1.0, 0.0)
            pick = pick.reshape(step * 2 * SLOTS, 2 * tokens).astype(BF16)
            rows = jnp.dot(pick, source, preferred_element_type=F32).astype(BF16)
            rows = rows.reshape(step, 2 * SLOTS, -1)
            for m in range(step):
                outb[(e + m) % 2, (e + m) // 2, q] = rows[m]
        inb[0, my_slot, q] = outb[0, self_dest, q]
        inb[1, my_slot, q] = outb[1, self_dest, q]

        @pl.loop(1, dests)
        def _(k):
            send_rows(0, k, q)

    for load in loads:
        load.wait()
    weights(0)
    for q in range(pairs):
        last = q == pairs - 1
        for way in range(2):
            source = 2 * q + way
            if not last or way == 1:
                pltpu.make_async_copy(ids_ref, idb.at[source], ids_r.at[source]).wait()
            if not last:
                pltpu.make_async_copy(tok.at[source], tok.at[source], tok_r.at[source]).wait()
            else:
                half = tok.at[line - 1, pl.ds(way * (tokens // 2), tokens // 2)]
                pltpu.make_async_copy(half, half, tok_r.at[source]).wait()
        if not last:
            start_hops(q + 2)
        pick_rows(q)
        if q == 0:
            weights(1)

    @pl.loop(1, dests)
    def _(k):
        d = (self_dest + k) % dests
        peer = (base2 + (d // 2) * stride2 + d % 2, xpos)
        pltpu.make_async_remote_copy(
            cnt_out.at[pl.ds(2 * d, 2)], cnt_in.at[my_slot], cnt_s, cnt_r,
            device_id=peer, device_id_type=MESH,
        ).start()


    @pl.loop(1, dests)
    def _(k):
        send_rows(1, k, None)

    cnt_in[my_slot] = cnt_out[pl.ds(2 * self_dest, 2)]

    def sent(i):
        return pl.ds(0, body + 16 * i)

    def gram(i):
        view = inb.at[i, pl.ds(0, dests - 1)]
        pltpu.make_async_copy(view, view, row_r.at[i]).wait()
        held = inb.at[i]
        rows = held[...].reshape(-1, columns)
        for b in range(blocks):
            product = lax.dot_general(
                rows[:, b * PANEL : (b + 1) * PANEL], rows[:, b * PANEL :],
                (((0,), (0,)), ((), ())), preferred_element_type=F32,
            ).astype(BF16)
            for c in range(b, blocks):
                t = upper.index((b, c))
                for p in range(n_dp):
                    gram_out[i, p, t * part_rows : (t + 1) * part_rows, :] = product[
                        p * part_rows : (p + 1) * part_rows,
                        (c - b) * PANEL : (c - b + 1) * PANEL,
                    ]
        if i == 1:
            view = cnt_in.at[pl.ds(0, dests - 1)]
            pltpu.make_async_copy(view, view, cnt_r).wait()
            count = jnp.sum(cnt_in[...], axis=0).reshape(16, PANEL).astype(BF16)
            for p in range(n_dp):
                gram_out[i, p, body:, :] = count
        for d in range(1, n_dp):
            other = (xpos + d) % n_dp
            pltpu.make_async_remote_copy(
                gram_out.at[i, other, sent(i)], gram_in.at[i, d - 1, sent(i)], rs_s.at[i, d - 1], rs_r.at[i, d - 1],
                device_id=(idx, other), device_id_type=MESH,
            ).start()

    def share(i):
        for d in range(1, n_dp):
            view = gram_in.at[i, d - 1, sent(i)]
            pltpu.make_async_copy(view, view, rs_r.at[i, d - 1]).wait()
        total = gram_out[i, xpos, sent(i)].astype(F32)
        for d in range(1, n_dp):
            total = total + gram_in[i, d - 1, sent(i)].astype(F32)
        whole[i, xpos] = total[:body].astype(BF16)
        for d in range(1, n_dp):
            other = (xpos + d) % n_dp
            pltpu.make_async_remote_copy(
                whole.at[i, xpos], whole.at[i, xpos], ag_s.at[i, d - 1], ag_r.at[i, xpos],
                device_id=(idx, other), device_id_type=MESH,
            ).start()
        if i == 1:
            total_cnt[...] = total[body:].reshape(2, 8, PANEL)

    def gathered(i):
        for d in range(1, n_dp):
            other = (xpos + d) % n_dp
            pltpu.make_async_copy(whole.at[i, other], whole.at[i, other], ag_r.at[i, other]).wait()

    gram(0)
    share(0)
    gram(1)
    share(1)
    gathered(0)
    gathered(1)

    for i in range(2):
        view = outb.at[i, pl.ds(0, dests - 1)]
        pltpu.make_async_copy(view, view, row_s.at[i]).wait()
        for d in range(n_dp - 1):
            view = gram_in.at[i, d, sent(i)]
            pltpu.make_async_copy(view, view, rs_s.at[i, d]).wait()
            pltpu.make_async_copy(whole.at[i, 0], whole.at[i, 0], ag_s.at[i, d]).wait()
    view = cnt_in.at[pl.ds(0, dests - 1)]
    pltpu.make_async_copy(view, view, cnt_s).wait()
    for copy in hops:
        copy.wait_send()
    view = idb.at[pl.ds(0, line - 1)]
    pltpu.make_async_copy(view, view, ids_s).wait()


def last_kernel(n_dp, w_ref, change, whole, cnt, q_ref, ww_ref, hg_ref, hess):
    columns = w_ref.shape[2]
    blocks = columns // PANEL
    part_rows = PANEL // n_dp
    weights = w_ref[0].astype(F32) + change[0].astype(F32)
    q_ref[0] = weights[:, :PANEL].astype(BF16)
    ww_ref[0] = weights[:, PANEL:].astype(BF16)
    inverse = 1.0 / jnp.sum(cnt[0, :1], axis=1, keepdims=True)
    for t, (b, c) in enumerate(upper_tiles(blocks)):
        for p in range(n_dp):
            hess[b * PANEL + p * part_rows : b * PANEL + (p + 1) * part_rows,
                 c * PANEL : (c + 1) * PANEL] = whole[0, p, t * part_rows : (t + 1) * part_rows, :]
    for c in range(blocks):
        low, high = c * PANEL, (c + 1) * PANEL
        out = jnp.dot(change[0, :, :high], hess[:high, low:high], preferred_element_type=F32)
        if high < columns:
            out = out + lax.dot_general(
                change[0, :, high:], hess[low:high, high:],
                (((1,), (1,)), ((), ())), preferred_element_type=F32,
            )
        hg_ref[0, :, low:high] = out * inverse


def per_device(tokens, expert_ids, weight_cols, uinv_panel, u_window, panel_index):
    n_expert, n_dp = lax.axis_size("expert"), lax.axis_size("dp")
    line = math.isqrt(n_expert // 2)
    dests = 2 * line
    rows, columns = weight_cols.shape[1:]
    n_tok, top_k = expert_ids.shape
    window = lax.dynamic_slice_in_dim(tokens, panel_index[0] * PANEL, columns, 1)
    blocks = columns // PANEL
    body = blocks * (blocks + 1) // 2 * (PANEL // n_dp)
    dma = pltpu.SemaphoreType.DMA
    vmem = pl.BlockSpec(memory_space=pltpu.VMEM)
    hbm = pl.BlockSpec(memory_space=pl.ANY)
    change, whole, cnt = pl.pallas_call(
        functools.partial(route_kernel, line, n_dp),
        out_shape=(
            jax.ShapeDtypeStruct((2, rows, columns), BF16),
            jax.ShapeDtypeStruct((2, n_dp, body, PANEL), BF16),
            jax.ShapeDtypeStruct((2, 8, PANEL), F32),
        ),
        in_specs=[vmem, vmem, hbm, hbm, hbm],
        out_specs=(vmem,) * 3,
        scratch_shapes=[
            pltpu.VMEM(weight_cols.shape, BF16),
            pltpu.VMEM(uinv_panel.shape, F32),
            pltpu.VMEM(u_window.shape, F32),
            pltpu.VMEM((line, n_tok, columns), BF16),
            pltpu.VMEM((line, top_k, n_tok), jnp.int32),
            pltpu.VMEM((2, dests, line // 2, 2 * SLOTS, columns), BF16),
            pltpu.VMEM((2, dests, line // 2, 2 * SLOTS, columns), BF16),
            pltpu.VMEM((2 * dests, 8, n_tok), F32),
            pltpu.VMEM((dests, 2, 8, n_tok), F32),
            pltpu.VMEM((2, n_dp, body + 16, PANEL), BF16),
            pltpu.VMEM((2, n_dp - 1, body + 16, PANEL), BF16),
            dma((3,)),
            dma((line,)), dma((line,)), dma, dma((line,)), dma((2,)), dma((2,)), dma, dma,
            dma((2, n_dp - 1)), dma((2, n_dp - 1)), dma((2, n_dp - 1)), dma((2, n_dp)),
        ],
        compiler_params=pltpu.CompilerParams(
            collective_id=0, has_side_effects=True, vmem_limit_bytes=32 * 1024 * 1024
        ),
    )(window, expert_ids.T, weight_cols, uinv_panel, u_window)

    def per_expert(*shape):
        return pl.BlockSpec((1,) + shape, lambda i: (i,) + (0,) * len(shape))

    return pl.pallas_call(
        functools.partial(last_kernel, n_dp),
        grid=(2,),
        out_shape=(
            jax.ShapeDtypeStruct((2, rows, PANEL), BF16),
            jax.ShapeDtypeStruct((2, rows, columns - PANEL), BF16),
            jax.ShapeDtypeStruct((2, rows, columns), F32),
        ),
        in_specs=[
            per_expert(rows, columns), per_expert(rows, columns),
            per_expert(n_dp, body, PANEL), per_expert(8, PANEL),
        ],
        out_specs=(per_expert(rows, PANEL), per_expert(rows, columns - PANEL), per_expert(rows, columns)),
        scratch_shapes=[pltpu.VMEM((columns, columns), BF16)],
        compiler_params=pltpu.CompilerParams(vmem_limit_bytes=16 * 1024 * 1024),
    )(weight_cols, change, whole, cnt)


def solution(mesh):
    placed = (
        P(("expert", "dp"), None),
        P(("expert", "dp"), None),
        P("expert", "dp", None),
        P("expert", None, None),
        P("expert", None, None),
        P(),
    )
    return jax.shard_map(
        per_device,
        mesh=mesh,
        in_specs=placed,
        out_specs=(P("expert", "dp", None), P("expert", "dp", None), P("expert", "dp", None)),
        check_vma=False,
    )
```

time: 108 us -> 95.2 us (0.88)
  Pallas kernels: 99.8 us -> 87.6 us
  local copies, waits for them, and re-layouts: 6.01 us -> 4.46 us
    pallas_call x1 -> x2, Pallas kernels: 99.8 us -> 87.6 us  [the longest x1 85.2 us: per_device(): pl.pallas_call(functools.partial(route_kernel, line, n_dp), out_shape=(ja...]
    unnamed x7 -> x10, local copies, waits for them, and re-layouts: 5.33 us -> 4.44 us
where the time goes in v2:
time: 95.2 us; the launch traced here: 93.5 us
  Pallas kernels  87.6 us (92%)
  local copies, waits for them, and re-layouts  4.46 us (5%)
  between operations  1.44 us (2%)
    pallas_call x1, Pallas kernels, per_device(): pl.pallas_call(functools.partial(route_kernel, line, n_dp), out_shape=(ja...  85.2 us
    unnamed x10, local copies, waits for them, and re-layouts  4.44 us
    pallas_call x1, Pallas kernels, per_device(): pl.pallas_call(functools.partial(last_kernel, n_dp), grid=(2,), out_shape...  2.34 us

profile of v2, /device:TPU:1, one launch (start us, length us, event | category | flops | bytes accessed | tf_op | source)
XLA Modules:
  0.0 93.5 jit_solution(822807556628052439)
XLA Ops:
  0.6 0.0 copy-start
  1.4 0.7 copy-done
  2.2 0.0 copy-start.1
  2.2 1.1 %copy-done.1 = bf16[2,256,640]{2,1,0:T(8,128)(2,1)S(1)} copy-done((bf16[2,256,640]{2,1,0:T(8,128)(2,1)S(1)}, bf16[2,256,640]{2,1,0:T(8,128)(2,1)}, u32[]{:S(2)}) %copy-start.1) | copy-done | bytes 655384
  3.3 0.0 copy-start.2
  3.3 1.0 %copy-done.2 = f32[2,128,512]{2,1,0:T(8,128)S(1)} copy-done((f32[2,128,512]{2,1,0:T(8,128)S(1)}, f32[2,128,512]{2,1,0:T(8,128)}, u32[]{:S(2)}) %copy-start.2) | copy-done | bytes 524312
  4.3 0.0 copy-start.3
  4.3 0.9 copy-done.3
  5.2 0.0 copy-start.4
  5.2 0.7 copy-done.4
  5.9 85.2 %shard_map.85 = (bf16[2,256,640]{2,1,0:T(8,128)(2,1)S(1)}, bf16[2,4,480,128]{3,2,1,0:T(8,128)(2,1)S(1)}, f32[2,8,128]{2,1,0:T(8,128)S(1)}) custom-call(bf16[128,640]{1,0:T(8,128)(2,1)S(1)} %constant_dynamic-slice_fusion.win_ref, s32[8,128]{1,0:T(8,128)S(1)} %bitcast.2, bf16[2,256,640]{2,1,0:T(8,128)(2,1)S(1)} %copy-done.1, f32[2,128,128]{2,1,0:T(8,128)S(1)} %copy-done.3, ...), custom_call_target="tpu_custom_call" | custom-call | tf_op jit(solution)/shard_map/pallas_call | solution.py:344
  91.1 2.3 %shard_map.86 = (bf16[2,256,128]{2,1,0:T(8,128)(2,1)}, bf16[2,256,512]{2,1,0:T(8,128)(2,1)}, f32[2,256,640]{2,1,0:T(8,128)}) custom-call(bf16[2,256,640]{2,1,0:T(8,128)(2,1)S(1)} %copy-done.1, bf16[2,256,640]{2,1,0:T(8,128)(2,1)S(1)} %get-tuple-element.6.change, bf16[2,4,480,128]{3,2,1,0:T(8,128)(2,1)S(1)} %get-tuple-element.7.whole, ...), custom_call_target="tpu_custom_call" | custom-call | tf_op jit(solution)/shard_map/pallas_call | solution.py:377
  (1 shorter events, 0.0 us)
Async XLA Ops:
  0.6 1.5 %copy-start = (bf16[128,7168]{1,0:T(8,128)(2,1)S(1)}, bf16[128,7168]{1,0:T(8,128)(2,1)}, u32[]{:S(2)}) copy-start(bf16[128,7168]{1,0:T(8,128)(2,1)} %param.6) | copy-start | bytes 5505028
  2.2 1.1 %copy-start.1 = (bf16[2,256,640]{2,1,0:T(8,128)(2,1)S(1)}, bf16[2,256,640]{2,1,0:T(8,128)(2,1)}, u32[]{:S(2)}) copy-start(bf16[2,256,640]{2,1,0:T(8,128)(2,1)} %w_ref.1) | copy-start | bytes 1966084
  3.3 1.0 %copy-start.2 = (f32[2,128,512]{2,1,0:T(8,128)S(1)}, f32[2,128,512]{2,1,0:T(8,128)}, u32[]{:S(2)}) copy-start(f32[2,128,512]{2,1,0:T(8,128)} %uw_hbm.1) | copy-start | bytes 1572868
  4.3 0.9 copy-start.3
  5.2 0.7 copy-start.4

commit v3 on v2

--- a/solution.py
+++ b/solution.py
@@ -10,6 +10,7 @@
 
 PANEL = 128
 SLOTS = 8
+PIECES = 4
 TWO_PI = 2.0 * math.pi
 HIGHEST = lax.Precision.HIGHEST
 MESH = pl.DeviceIdType.MESH
@@ -30,8 +31,9 @@
     return angle * series
 
 
-def upper_tiles(blocks):
-    return [(b, c) for b in range(blocks) for c in range(b, blocks)]
+def tiles_of(blocks):
+    last = blocks - 1
+    return [(b, c) for b in range(last) for c in range(b, last)] + [(last, c) for c in range(blocks)]
 
 
 def route_kernel(
@@ -50,9 +52,11 @@
     pairs = line // 2
     columns = w_ref.shape[2]
     blocks = columns // PANEL
-    upper = upper_tiles(blocks)
+    tiles = tiles_of(blocks)
+    main = columns - PANEL
     part_rows = PANEL // n_dp
-    body = len(upper) * part_rows
+    body = len(tiles) * part_rows
+    body_main = (len(tiles) - blocks) * part_rows
     tokens = tok.shape[1]
     own = line - 2
 
@@ -114,25 +118,29 @@
                 device_id=(base1 + at * stride1, xpos), device_id_type=MESH,
             ).start()
 
-    def hop(source, target, way, far):
-        rows = pl.ds(way * (tokens // 2), tokens // 2) if far else pl.ds(0, tokens)
-        sem = 2 * pairs - 2 + way if far else target
-        return pltpu.make_async_remote_copy(
-            tok.at[source, rows], tok.at[target, rows], tok_s.at[sem], tok_r.at[sem],
+    piece_rows = tokens // PIECES
+
+    def pieces_of(way, far):
+        return range(way * PIECES // 2, (way + 1) * PIECES // 2) if far else range(PIECES)
+
+    hops = []
+
+    def start_hop(step, way, piece):
+        source = own if step == 1 else 2 * (step - 2) + way
+        target = line - 1 if step == pairs else 2 * (step - 1) + way
+        rows = pl.ds(piece * piece_rows, piece_rows)
+        copy = pltpu.make_async_remote_copy(
+            tok.at[source, rows], tok.at[target, rows],
+            tok_s.at[target, piece], tok_r.at[target, piece],
             device_id=right if way == 0 else left, device_id_type=MESH,
         )
-
-    hops = []
-
-    def start_hops(step):
+        copy.start()
+        hops.append(copy)
+
+    for piece in range(PIECES):
         for way in range(2):
-            far = step == pairs
-            source = own if step == 1 else 2 * (step - 2) + way
-            copy = hop(source, line - 1 if far else 2 * (step - 1) + way, way, far)
-            copy.start()
-            hops.append(copy)
-
-    start_hops(1)
+            if piece in pieces_of(way, pairs == 1):
+                start_hop(1, way, piece)
 
     def weights(i):
         panel = w_ref[i, :, :PANEL].astype(F32)
@@ -157,15 +165,16 @@
     slot_of = lax.broadcasted_iota(jnp.int32, (2 * SLOTS, 2 * tokens), 0).astype(F32)
     cnt_out[...] = jnp.zeros_like(cnt_out)
 
-    def send_rows(i, k, q):
+    def cut(group):
+        return (pl.ds(0, columns), pl.ds(0, main), pl.ds(main, PANEL))[group]
+
+    def send_rows(group, k, q):
         d = (self_dest + k) % dests
-        peer = (base2 + (d // 2) * stride2 + d % 2, xpos)
-        if q is None:
-            src, dst = outb.at[i, d], inb.at[i, my_slot]
-        else:
-            src, dst = outb.at[i, d, q], inb.at[i, my_slot, q]
+        i = 1 if group else 0
         pltpu.make_async_remote_copy(
-            src, dst, row_s.at[i], row_r.at[i], device_id=peer, device_id_type=MESH
+            outb.at[i, d, q, :, cut(group)], inb.at[i, my_slot, q, :, cut(group)],
+            row_s.at[group], row_r.at[group],
+            device_id=(base2 + (d // 2) * stride2 + d % 2, xpos), device_id_type=MESH,
         ).start()
 
     def pick_rows(q):
@@ -193,25 +202,20 @@
         def _(k):
             send_rows(0, k, q)
 
-    for load in loads:
-        load.wait()
-    weights(0)
     for q in range(pairs):
         last = q == pairs - 1
-        for way in range(2):
-            source = 2 * q + way
-            if not last or way == 1:
+        for piece in range(PIECES):
+            for way in range(2):
+                if piece in pieces_of(way, last):
+                    source = line - 1 if last else 2 * q + way
+                    held = tok.at[source, pl.ds(piece * piece_rows, piece_rows)]
+                    pltpu.make_async_copy(held, held, tok_r.at[source, piece]).wait()
+                    if not last and piece in pieces_of(way, q + 2 == pairs):
+                        start_hop(q + 2, way, piece)
+        for source in range(2 * q, 2 * q + 2):
+            if source != own:
                 pltpu.make_async_copy(ids_ref, idb.at[source], ids_r.at[source]).wait()
-            if not last:
-                pltpu.make_async_copy(tok.at[source], tok.at[source], tok_r.at[source]).wait()
-            else:
-                half = tok.at[line - 1, pl.ds(way * (tokens // 2), tokens // 2)]
-                pltpu.make_async_copy(half, half, tok_r.at[source]).wait()
-        if not last:
-            start_hops(q + 2)
         pick_rows(q)
-        if q == 0:
-            weights(1)
 
     @pl.loop(1, dests)
     def _(k):
@@ -222,34 +226,42 @@
             device_id=peer, device_id_type=MESH,
         ).start()
 
-
-    @pl.loop(1, dests)
-    def _(k):
-        send_rows(1, k, None)
+    for group in (1, 2):
+
+        @pl.loop(1, dests)
+        def _(k):
+            send_rows(group, k, slice(None))
 
     cnt_in[my_slot] = cnt_out[pl.ds(2 * self_dest, 2)]
 
-    def sent(i):
-        return pl.ds(0, body + 16 * i)
-
-    def gram(i):
-        view = inb.at[i, pl.ds(0, dests - 1)]
-        pltpu.make_async_copy(view, view, row_r.at[i]).wait()
-        held = inb.at[i]
-        rows = held[...].reshape(-1, columns)
-        for b in range(blocks):
+    def wait_rows(group, sem):
+        view = inb.at[1 if group else 0, pl.ds(0, dests - 1), :, :, cut(group)]
+        pltpu.make_async_copy(view, view, sem.at[group]).wait()
+
+    def part(group, counts=True):
+        first, size = ((0, body), (0, body_main), (body_main, body - body_main))[group]
+        return pl.ds(first, size + (16 if counts and group == 2 else 0))
+
+    def gram(group):
+        wait_rows(group, row_r)
+        i = 1 if group else 0
+        wide = main if group == 1 else columns
+        rows = inb[i, :, :, :, pl.ds(0, wide)].reshape(-1, wide)
+        first = blocks - 1 if group == 2 else 0
+        for b in range(first, blocks - 1 if group == 1 else blocks):
+            start, stop = (0, columns) if b == blocks - 1 else (b * PANEL, main)
             product = lax.dot_general(
-                rows[:, b * PANEL : (b + 1) * PANEL], rows[:, b * PANEL :],
+                rows[:, b * PANEL : (b + 1) * PANEL], rows[:, start:stop],
                 (((0,), (0,)), ((), ())), preferred_element_type=F32,
             ).astype(BF16)
-            for c in range(b, blocks):
-                t = upper.index((b, c))
+            for c in range(start // PANEL, stop // PANEL):
+                t = tiles.index((b, c))
                 for p in range(n_dp):
                     gram_out[i, p, t * part_rows : (t + 1) * part_rows, :] = product[
                         p * part_rows : (p + 1) * part_rows,
-                        (c - b) * PANEL : (c - b + 1) * PANEL,
+                        c * PANEL - start : (c + 1) * PANEL - start,
                     ]
-        if i == 1:
+        if group == 2:
             view = cnt_in.at[pl.ds(0, dests - 1)]
             pltpu.make_async_copy(view, view, cnt_r).wait()
             count = jnp.sum(cnt_in[...], axis=0).reshape(16, PANEL).astype(BF16)
@@ -258,46 +270,56 @@
         for d in range(1, n_dp):
             other = (xpos + d) % n_dp
             pltpu.make_async_remote_copy(
-                gram_out.at[i, other, sent(i)], gram_in.at[i, d - 1, sent(i)], rs_s.at[i, d - 1], rs_r.at[i, d - 1],
+                gram_out.at[i, other, part(group)], gram_in.at[i, d - 1, part(group)],
+                rs_s.at[group, d - 1], rs_r.at[group, d - 1],
                 device_id=(idx, other), device_id_type=MESH,
             ).start()
 
-    def share(i):
+    def wait_shares(group, sem):
         for d in range(1, n_dp):
-            view = gram_in.at[i, d - 1, sent(i)]
-            pltpu.make_async_copy(view, view, rs_r.at[i, d - 1]).wait()
-        total = gram_out[i, xpos, sent(i)].astype(F32)
+            view = gram_in.at[1 if group else 0, d - 1, part(group)]
+            pltpu.make_async_copy(view, view, sem.at[group, d - 1]).wait()
+
+    def share(group):
+        wait_shares(group, rs_r)
+        i = 1 if group else 0
+        total = gram_out[i, xpos, part(group)].astype(F32)
         for d in range(1, n_dp):
-            total = total + gram_in[i, d - 1, sent(i)].astype(F32)
-        whole[i, xpos] = total[:body].astype(BF16)
+            total = total + gram_in[i, d - 1, part(group)].astype(F32)
+        mine = part(group, False)
+        whole[i, xpos, mine] = total[: mine.size].astype(BF16)
         for d in range(1, n_dp):
             other = (xpos + d) % n_dp
             pltpu.make_async_remote_copy(
-                whole.at[i, xpos], whole.at[i, xpos], ag_s.at[i, d - 1], ag_r.at[i, xpos],
+                whole.at[i, xpos, mine], whole.at[i, xpos, mine],
+                ag_s.at[group, d - 1], ag_r.at[group, d - 1],
                 device_id=(idx, other), device_id_type=MESH,
             ).start()
-        if i == 1:
-            total_cnt[...] = total[body:].reshape(2, 8, PANEL)
-
-    def gathered(i):
+        if group == 2:
+            total_cnt[...] = total[mine.size :].reshape(2, 8, PANEL)
+
+    def wait_whole(group, sem):
         for d in range(1, n_dp):
-            other = (xpos + d) % n_dp
-            pltpu.make_async_copy(whole.at[i, other], whole.at[i, other], ag_r.at[i, other]).wait()
-
+            view = whole.at[1 if group else 0, (xpos + n_dp - d) % n_dp, part(group, False)]
+            pltpu.make_async_copy(view, view, sem.at[group, d - 1]).wait()
+
+    for load in loads:
+        load.wait()
+    weights(0)
+    weights(1)
     gram(0)
     share(0)
     gram(1)
+    gram(2)
     share(1)
-    gathered(0)
-    gathered(1)
-
-    for i in range(2):
-        view = outb.at[i, pl.ds(0, dests - 1)]
-        pltpu.make_async_copy(view, view, row_s.at[i]).wait()
-        for d in range(n_dp - 1):
-            view = gram_in.at[i, d, sent(i)]
-            pltpu.make_async_copy(view, view, rs_s.at[i, d]).wait()
-            pltpu.make_async_copy(whole.at[i, 0], whole.at[i, 0], ag_s.at[i, d]).wait()
+    share(2)
+    for group in range(3):
+        wait_whole(group, ag_r)
+
+    for group in range(3):
+        wait_rows(group, row_s)
+        wait_shares(group, rs_s)
+        wait_whole(group, ag_s)
     view = cnt_in.at[pl.ds(0, dests - 1)]
     pltpu.make_async_copy(view, view, cnt_s).wait()
     for copy in hops:
@@ -314,19 +336,22 @@
     q_ref[0] = weights[:, :PANEL].astype(BF16)
     ww_ref[0] = weights[:, PANEL:].astype(BF16)
     inverse = 1.0 / jnp.sum(cnt[0, :1], axis=1, keepdims=True)
-    for t, (b, c) in enumerate(upper_tiles(blocks)):
+    main = columns - PANEL
+    for t, (b, c) in enumerate(tiles_of(blocks)):
         for p in range(n_dp):
             hess[b * PANEL + p * part_rows : b * PANEL + (p + 1) * part_rows,
                  c * PANEL : (c + 1) * PANEL] = whole[0, p, t * part_rows : (t + 1) * part_rows, :]
-    for c in range(blocks):
+    def across(left, right):
+        return lax.dot_general(left, right, (((1,), (1,)), ((), ())), preferred_element_type=F32)
+
+    for c in range(blocks - 1):
         low, high = c * PANEL, (c + 1) * PANEL
         out = jnp.dot(change[0, :, :high], hess[:high, low:high], preferred_element_type=F32)
-        if high < columns:
-            out = out + lax.dot_general(
-                change[0, :, high:], hess[low:high, high:],
-                (((1,), (1,)), ((), ())), preferred_element_type=F32,
-            )
+        out = out + jnp.dot(change[0, :, main:], hess[main:, low:high], preferred_element_type=F32)
+        if high < main:
+            out = out + across(change[0, :, high:main], hess[low:high, high:main])
         hg_ref[0, :, low:high] = out * inverse
+    hg_ref[0, :, main:] = across(change[0], hess[main:]) * inverse
 
 
 def per_device(tokens, expert_ids, weight_cols, uinv_panel, u_window, panel_index):
@@ -363,11 +388,11 @@
             pltpu.VMEM((2, n_dp, body + 16, PANEL), BF16),
             pltpu.VMEM((2, n_dp - 1, body + 16, PANEL), BF16),
             dma((3,)),
-            dma((line,)), dma((line,)), dma, dma((line,)), dma((2,)), dma((2,)), dma, dma,
-            dma((2, n_dp - 1)), dma((2, n_dp - 1)), dma((2, n_dp - 1)), dma((2, n_dp)),
+            dma((line, PIECES)), dma((line, PIECES)), dma, dma((line,)), dma((3,)), dma((3,)), dma, dma,
+            dma((3, n_dp - 1)), dma((3, n_dp - 1)), dma((3, n_dp - 1)), dma((3, n_dp - 1)),
         ],
         compiler_params=pltpu.CompilerParams(
-            collective_id=0, has_side_effects=True, vmem_limit_bytes=32 * 1024 * 1024
+            collective_id=0, has_side_effects=True, vmem_limit_bytes=56 * 1024 * 1024
         ),
     )(window, expert_ids.T, weight_cols, uinv_panel, u_window)
 

time: 95.2 us -> 86.4 us (0.908); the launches traced: 93.5 us -> 86.1 us
  Pallas kernels: 87.6 us -> 80.2 us
    pallas_call x1, Pallas kernels: 85.2 us -> 78 us  [per_device(): pl.pallas_call(functools.partial(route_kernel, line, n_dp), out_shape=(ja...]
where the time goes in v3:
time: 86.4 us; the launch traced here: 86.1 us
  Pallas kernels  80.2 us (93%)
  local copies, waits for them, and re-layouts  4.37 us (5%)
  between operations  1.47 us (2%)
    pallas_call x1, Pallas kernels, per_device(): pl.pallas_call(functools.partial(route_kernel, line, n_dp), out_shape=(ja...  78 us
    unnamed x10, local copies, waits for them, and re-layouts  3.69 us
    pallas_call x1, Pallas kernels, per_device(): pl.pallas_call(functools.partial(last_kernel, n_dp), grid=(2,), out_shape...  2.28 us

profile of v3, /device:TPU:1, one launch (start us, length us, event | category | flops | bytes accessed | tf_op | source)
XLA Modules:
  0.0 86.1 jit_solution(6598948539561557706)
XLA Ops:
  0.6 0.0 copy-start
  0.6 0.0 copy-start.1
  1.5 0.7 copy-done
  2.2 0.7 constant_dynamic-slice_fusion.win_ref
  2.8 78.0 %shard_map.85 = (bf16[2,256,640]{2,1,0:T(8,128)(2,1)}, bf16[2,4,480,128]{3,2,1,0:T(8,128)(2,1)}, f32[2,8,128]{2,1,0:T(8,128)}) custom-call(bf16[128,640]{1,0:T(8,128)(2,1)} %constant_dynamic-slice_fusion.win_ref, s32[8,128]{1,0:T(8,128)} %bitcast.2, bf16[2,256,640]{2,1,0:T(8,128)(2,1)} %w_ref.1, f32[2,128,128]{2,1,0:T(8,128)} %uinv_hbm.1, f32[2,128,512]{2,1,0:T(8,128)} %uw_hbm.1), custom_call_target="tpu_custom_call" | custom-call | tf_op jit(solution)/shard_map/pallas_call | solution.py:369
  80.8 0.0 copy-done.1
  80.8 0.0 copy-start.2
  80.8 1.2 %copy-done.2 = bf16[2,4,480,128]{3,2,1,0:T(8,128)(2,1)S(1)} copy-done((bf16[2,4,480,128]{3,2,1,0:T(8,128)(2,1)S(1)}, bf16[2,4,480,128]{3,2,1,0:T(8,128)(2,1)}, u32[]{:S(2)}) %copy-start.2) | copy-done | bytes 983064
  82.0 0.0 copy-start.3
  82.0 1.1 %copy-done.3 = bf16[2,256,640]{2,1,0:T(8,128)(2,1)S(1)} copy-done((bf16[2,256,640]{2,1,0:T(8,128)(2,1)S(1)}, bf16[2,256,640]{2,1,0:T(8,128)(2,1)}, u32[]{:S(2)}) %copy-start.3) | copy-done | bytes 655384
  83.1 0.0 copy-start.4
  83.1 0.7 copy-done.4
  83.8 2.3 %shard_map.86 = (bf16[2,256,128]{2,1,0:T(8,128)(2,1)}, bf16[2,256,512]{2,1,0:T(8,128)(2,1)}, f32[2,256,640]{2,1,0:T(8,128)}) custom-call(bf16[2,256,640]{2,1,0:T(8,128)(2,1)S(1)} %copy-done.1, bf16[2,256,640]{2,1,0:T(8,128)(2,1)S(1)} %copy-done.3, bf16[2,4,480,128]{3,2,1,0:T(8,128)(2,1)S(1)} %copy-done.2, f32[2,8,128]{2,1,0:T(8,128)S(1)} %copy-done.4), custom_call_target="tpu_custom_call" | custom-call | tf_op jit(solution)/shard_map/pallas_call | solution.py:402
Async XLA Ops:
  0.6 1.5 %copy-start = (bf16[128,7168]{1,0:T(8,128)(2,1)S(1)}, bf16[128,7168]{1,0:T(8,128)(2,1)}, u32[]{:S(2)}) copy-start(bf16[128,7168]{1,0:T(8,128)(2,1)} %param.6) | copy-start | bytes 5505028
  0.6 80.2 %copy-start.1 = (bf16[2,256,640]{2,1,0:T(8,128)(2,1)S(1)}, bf16[2,256,640]{2,1,0:T(8,128)(2,1)}, u32[]{:S(2)}) copy-start(bf16[2,256,640]{2,1,0:T(8,128)(2,1)} %w_ref.1) | copy-start | bytes 1966084
  80.8 1.2 %copy-start.2 = (bf16[2,4,480,128]{3,2,1,0:T(8,128)(2,1)S(1)}, bf16[2,4,480,128]{3,2,1,0:T(8,128)(2,1)}, u32[]{:S(2)}) copy-start(bf16[2,4,480,128]{3,2,1,0:T(8,128)(2,1)} %get-tuple-element.7.whole) | copy-start | bytes 2949124
  82.0 1.1 %copy-start.3 = (bf16[2,256,640]{2,1,0:T(8,128)(2,1)S(1)}, bf16[2,256,640]{2,1,0:T(8,128)(2,1)}, u32[]{:S(2)}) copy-start(bf16[2,256,640]{2,1,0:T(8,128)(2,1)} %get-tuple-element.6.change) | copy-start | bytes 1966084
  83.1 0.7 copy-start.4

commit v4 on v3

--- a/solution.py
+++ b/solution.py
@@ -198,9 +198,11 @@
         inb[0, my_slot, q] = outb[0, self_dest, q]
         inb[1, my_slot, q] = outb[1, self_dest, q]
 
-        @pl.loop(1, dests)
-        def _(k):
-            send_rows(0, k, q)
+        for r in ([q - 1] if q < pairs - 1 else [q - 1, q]) if q else []:
+
+            @pl.loop(1, dests)
+            def _(k):
+                send_rows(0, k, r)
 
     for q in range(pairs):
         last = q == pairs - 1
@@ -226,11 +228,9 @@
             device_id=peer, device_id_type=MESH,
         ).start()
 
-    for group in (1, 2):
-
-        @pl.loop(1, dests)
-        def _(k):
-            send_rows(group, k, slice(None))
+    @pl.loop(1, dests)
+    def _(k):
+        send_rows(1, k, pl.ds(0, pairs))
 
     cnt_in[my_slot] = cnt_out[pl.ds(2 * self_dest, 2)]
 
@@ -309,6 +309,11 @@
     weights(1)
     gram(0)
     share(0)
+
+    @pl.loop(1, dests)
+    def _(k):
+        send_rows(2, k, pl.ds(0, pairs))
+
     gram(1)
     gram(2)
     share(1)
@@ -413,7 +418,7 @@
         ],
         out_specs=(per_expert(rows, PANEL), per_expert(rows, columns - PANEL), per_expert(rows, columns)),
         scratch_shapes=[pltpu.VMEM((columns, columns), BF16)],
-        compiler_params=pltpu.CompilerParams(vmem_limit_bytes=16 * 1024 * 1024),
+        compiler_params=pltpu.CompilerParams(vmem_limit_bytes=56 * 1024 * 1024),
     )(weight_cols, change, whole, cnt)
 
 

time: 86.4 us -> 83.4 us (0.965)
  local copies, waits for them, and re-layouts: 4.37 us -> 1.41 us
    unnamed x10 -> x2, local copies, waits for them, and re-layouts: 3.69 us -> 0.73 us
    pallas_call x1, Pallas kernels: 2.28 us -> 3.56 us  [per_device(): pl.pallas_call(functools.partial(last_kernel, n_dp), grid=(2,), out_shape...]
    pallas_call x1, Pallas kernels: 78 us -> 76.8 us  [per_device(): pl.pallas_call(functools.partial(route_kernel, line, n_dp), out_shape=(ja...]
where the time goes in v4:
time: 83.4 us; the launch traced here: 83.2 us
  Pallas kernels  80.4 us (96%)
  between operations  1.43 us (2%)
  local copies, waits for them, and re-layouts  1.41 us (2%)
    pallas_call x1, Pallas kernels, per_device(): pl.pallas_call(functools.partial(route_kernel, line, n_dp), out_shape=(ja...  76.8 us
    pallas_call x1, Pallas kernels, per_device(): pl.pallas_call(functools.partial(last_kernel, n_dp), grid=(2,), out_shape...  3.56 us

profile of v4, /device:TPU:1, one launch (start us, length us, event | category | flops | bytes accessed | tf_op | source)
XLA Modules:
  0.0 83.2 jit_solution(12121819114367979891)
XLA Ops:
  0.6 0.0 copy-start
  1.4 0.7 copy-done
  2.2 0.7 constant_dynamic-slice_fusion.win_ref
  2.8 76.8 %shard_map.85 = (bf16[2,256,640]{2,1,0:T(8,128)(2,1)}, bf16[2,4,480,128]{3,2,1,0:T(8,128)(2,1)}, f32[2,8,128]{2,1,0:T(8,128)}) custom-call(bf16[128,640]{1,0:T(8,128)(2,1)} %constant_dynamic-slice_fusion.win_ref, s32[8,128]{1,0:T(8,128)} %bitcast.2, bf16[2,256,640]{2,1,0:T(8,128)(2,1)} %w_ref.1, f32[2,128,128]{2,1,0:T(8,128)} %uinv_hbm.1, f32[2,128,512]{2,1,0:T(8,128)} %uw_hbm.1), custom_call_target="tpu_custom_call" | custom-call | tf_op jit(solution)/shard_map/pallas_call | solution.py:374
  79.7 3.6 %shard_map.86 = (bf16[2,256,128]{2,1,0:T(8,128)(2,1)}, bf16[2,256,512]{2,1,0:T(8,128)(2,1)}, f32[2,256,640]{2,1,0:T(8,128)}) custom-call(bf16[2,256,640]{2,1,0:T(8,128)(2,1)} %w_ref.1, bf16[2,256,640]{2,1,0:T(8,128)(2,1)} %get-tuple-element.6.change, bf16[2,4,480,128]{3,2,1,0:T(8,128)(2,1)} %get-tuple-element.7.whole, f32[2,8,128]{2,1,0:T(8,128)} %get-tuple-element.8.cnt), custom_call_target="tpu_custom_call" | custom-call | tf_op jit(solution)/shard_map/pallas_call | solution.py:407
Async XLA Ops:
  0.6 1.5 %copy-start = (bf16[128,7168]{1,0:T(8,128)(2,1)S(1)}, bf16[128,7168]{1,0:T(8,128)(2,1)}, u32[]{:S(2)}) copy-start(bf16[128,7168]{1,0:T(8,128)(2,1)} %param.6) | copy-start | bytes 5505028

commit v5 on v4

--- a/solution.py
+++ b/solution.py
@@ -109,15 +109,6 @@
     right = (base1 + ((place1 + 1) % line) * stride1, xpos)
     left = (base1 + ((place1 + line - 1) % line) * stride1, xpos)
 
-    for step in range(1, pairs + 1):
-        for way in range(1 if step == pairs else 2):
-            slot = 2 * (step - 1) + way + (1 if step == pairs else 0)
-            at = (place1 + (step if way == 0 else line - step)) % line
-            pltpu.make_async_remote_copy(
-                ids_ref, idb.at[slot], ids_s, ids_r.at[slot],
-                device_id=(base1 + at * stride1, xpos), device_id_type=MESH,
-            ).start()
-
     piece_rows = tokens // PIECES
 
     def pieces_of(way, far):
@@ -141,6 +132,15 @@
         for way in range(2):
             if piece in pieces_of(way, pairs == 1):
                 start_hop(1, way, piece)
+
+    for step in range(1, pairs + 1):
+        for way in range(1 if step == pairs else 2):
+            slot = 2 * (step - 1) + way + (1 if step == pairs else 0)
+            at = (place1 + (step if way == 0 else line - step)) % line
+            pltpu.make_async_remote_copy(
+                ids_ref, idb.at[slot], ids_s, ids_r.at[slot],
+                device_id=(base1 + at * stride1, xpos), device_id_type=MESH,
+            ).start()
 
     def weights(i):
         panel = w_ref[i, :, :PANEL].astype(F32)
@@ -185,7 +185,8 @@
         rank = jnp.dot(member.astype(BF16), before, preferred_element_type=F32)
         rank = jnp.where(member > 0.5, rank, -1.0)
         half = member[:, :tokens] + member[:, tokens:]
-        cnt_out[...] += jnp.broadcast_to(half[:, None, :], cnt_out.shape)
+        for d in range(dests):
+            cnt_out[d, 0:2] += half[2 * d : 2 * d + 2]
         source = tok[pl.ds(2 * q, 2)].reshape(2 * tokens, columns)
         step = min(8, 2 * dests)
         for e in range(0, 2 * dests, step):
@@ -224,7 +225,7 @@
         d = (self_dest + k) % dests
         peer = (base2 + (d // 2) * stride2 + d % 2, xpos)
         pltpu.make_async_remote_copy(
-            cnt_out.at[pl.ds(2 * d, 2)], cnt_in.at[my_slot], cnt_s, cnt_r,
+            cnt_out.at[d], cnt_in.at[my_slot], cnt_s, cnt_r,
             device_id=peer, device_id_type=MESH,
         ).start()
 
@@ -232,7 +233,7 @@
     def _(k):
         send_rows(1, k, pl.ds(0, pairs))
 
-    cnt_in[my_slot] = cnt_out[pl.ds(2 * self_dest, 2)]
+    cnt_in[my_slot] = cnt_out[self_dest]
 
     def wait_rows(group, sem):
         view = inb.at[1 if group else 0, pl.ds(0, dests - 1), :, :, cut(group)]
@@ -264,7 +265,8 @@
         if group == 2:
             view = cnt_in.at[pl.ds(0, dests - 1)]
             pltpu.make_async_copy(view, view, cnt_r).wait()
-            count = jnp.sum(cnt_in[...], axis=0).reshape(16, PANEL).astype(BF16)
+            count = jnp.sum(cnt_in[...], axis=0)
+            count = jnp.concatenate([count, jnp.zeros_like(count)], axis=0).astype(BF16)
             for p in range(n_dp):
                 gram_out[i, p, body:, :] = count
         for d in range(1, n_dp):
@@ -296,7 +298,9 @@
                 device_id=(idx, other), device_id_type=MESH,
             ).start()
         if group == 2:
-            total_cnt[...] = total[mine.size :].reshape(2, 8, PANEL)
+            for expert in range(2):
+                row = total[mine.size + expert : mine.size + expert + 1]
+                total_cnt[expert] = jnp.broadcast_to(row, (8, PANEL))
 
     def wait_whole(group, sem):
         for d in range(1, n_dp):
@@ -388,8 +392,8 @@
             pltpu.VMEM((line, top_k, n_tok), jnp.int32),
             pltpu.VMEM((2, dests, line // 2, 2 * SLOTS, columns), BF16),
             pltpu.VMEM((2, dests, line // 2, 2 * SLOTS, columns), BF16),
-            pltpu.VMEM((2 * dests, 8, n_tok), F32),
-            pltpu.VMEM((dests, 2, 8, n_tok), F32),
+            pltpu.VMEM((dests, 8, n_tok), F32),
+            pltpu.VMEM((dests, 8, n_tok), F32),
             pltpu.VMEM((2, n_dp, body + 16, PANEL), BF16),
             pltpu.VMEM((2, n_dp - 1, body + 16, PANEL), BF16),
             dma((3,)),

time: 83.4 us -> 83.5 us (level)
  no operation moved by 1% of the time
where the time goes in v5:
time: 83.5 us; the launch traced here: 83.1 us
  Pallas kernels  80.3 us (96%)
  between operations  1.43 us (2%)
  local copies, waits for them, and re-layouts  1.41 us (2%)
    pallas_call x1, Pallas kernels, per_device(): pl.pallas_call(functools.partial(route_kernel, line, n_dp), out_shape=(ja...  76.7 us
    pallas_call x1, Pallas kernels, per_device(): pl.pallas_call(functools.partial(last_kernel, n_dp), grid=(2,), out_shape...  3.56 us

profile of v5, /device:TPU:1, one launch (start us, length us, event | category | flops | bytes accessed | tf_op | source)
XLA Modules:
  0.0 83.1 jit_solution(255595313975375033)
XLA Ops:
  0.6 0.0 copy-start
  1.4 0.7 copy-done
  2.2 0.7 constant_dynamic-slice_fusion.win_ref
  2.8 76.7 %shard_map.85 = (bf16[2,256,640]{2,1,0:T(8,128)(2,1)}, bf16[2,4,480,128]{3,2,1,0:T(8,128)(2,1)}, f32[2,8,128]{2,1,0:T(8,128)}) custom-call(bf16[128,640]{1,0:T(8,128)(2,1)} %constant_dynamic-slice_fusion.win_ref, s32[8,128]{1,0:T(8,128)} %bitcast.2, bf16[2,256,640]{2,1,0:T(8,128)(2,1)} %w_ref.1, f32[2,128,128]{2,1,0:T(8,128)} %uinv_hbm.1, f32[2,128,512]{2,1,0:T(8,128)} %uw_hbm.1), custom_call_target="tpu_custom_call" | custom-call | tf_op jit(solution)/shard_map/pallas_call | solution.py:378
  79.6 3.6 %shard_map.86 = (bf16[2,256,128]{2,1,0:T(8,128)(2,1)}, bf16[2,256,512]{2,1,0:T(8,128)(2,1)}, f32[2,256,640]{2,1,0:T(8,128)}) custom-call(bf16[2,256,640]{2,1,0:T(8,128)(2,1)} %w_ref.1, bf16[2,256,640]{2,1,0:T(8,128)(2,1)} %get-tuple-element.6.change, bf16[2,4,480,128]{3,2,1,0:T(8,128)(2,1)} %get-tuple-element.7.whole, f32[2,8,128]{2,1,0:T(8,128)} %get-tuple-element.8.cnt), custom_call_target="tpu_custom_call" | custom-call | tf_op jit(solution)/shard_map/pallas_call | solution.py:411
Async XLA Ops:
  0.6 1.5 %copy-start = (bf16[128,7168]{1,0:T(8,128)(2,1)S(1)}, bf16[128,7168]{1,0:T(8,128)(2,1)}, u32[]{:S(2)}) copy-start(bf16[128,7168]{1,0:T(8,128)(2,1)} %param.6) | copy-start | bytes 5505028
